TPU v7x, 32 devices: a whole 2x2x4 slice. The times are simulated.
32 devices in a mesh: ctx: 16 (over z, x, core), head: 2 (over y).
Axes of the slice: x: 2, y: 2, z: 4, core: 2. Of those that a mesh axis runs over, the one named last changes fastest.
Arguments:
- queries: bfloat16 [4096, 1024], P('ctx', 'head'), may hold values from -6 to 6
- key_rows: bfloat16 [4096, 256], P('ctx', 'head'), may hold values from -6 to 6
- value_rows: bfloat16 [4096, 256], P('ctx', 'head'), may hold values from -6 to 6
- attn_out: bfloat16 [4096, 1024], P('ctx', 'head'), may hold values from -6 to 6
- out_grad: bfloat16 [4096, 1024], P('ctx', 'head'), may hold values from -6 to 6
- log_sums: float32 [8, 4096], P('head', 'ctx'), may hold values from 4.5 to 6
- block_picks: int32 [32, 8, 3], P('ctx', 'head'), may hold values from 0 to 3, all different within a row
- query_weight: bfloat16 [4096, 1024], P('ctx', 'head'), may hold values from -0.21875 to 0.21875
- key_weight: bfloat16 [4096, 256], P('ctx', 'head'), may hold values from -0.21875 to 0.21875
- value_weight: bfloat16 [4096, 256], P('ctx', 'head'), may hold values from -0.21875 to 0.21875
Outputs:
- input_grad: bfloat16 [4096, 4096], P('ctx', 'head')
Inputs may be any that keep to these rules, and one draw needn't show every extreme that they name: `block_picks`: in each row (query block, query head) the 3 entries differ; entry m selects the block m + 1 blocks before the query's block, and selections before the sequence's start select nothing.
All inputs are finite; a program needn't handle non-finite values.
Results may differ from a plain program's by a relative error of at most 0.013.
Values may be sent and summed in bfloat16 or wider, within the bound.
A program may use at most 64 MiB of HBM per device.

v0:
```python
import math

import jax
import jax.numpy as jnp
from jax import lax
from jax.sharding import PartitionSpec as P

BLK = 128


def passed_along(x, axis, by):
    devices = lax.axis_size(axis)
    pairs = [(i, i + by) for i in range(devices) if 0 <= i + by < devices]
    return lax.ppermute(x, axis, pairs)


def block_grads(
    query_blocks,
    grad_blocks,
    log_part,
    delta_part,
    pick_part,
    query_first,
    key_table,
    value_table,
    key_first,
):
    blocks, width, group, head_dim = query_blocks.shape
    table_blocks = key_table.shape[0]
    scaling = 1.0 / math.sqrt(head_dim)
    offsets = jnp.concatenate([jnp.zeros((blocks, group, 1), jnp.int32), pick_part + 1], axis=2)
    query_ids = query_first + jnp.arange(blocks, dtype=jnp.int32)
    key_block = query_ids[:, None, None] - offsets
    table_index = key_block - key_first
    usable = (table_index >= 0) & (table_index < table_blocks) & (key_block >= 0)
    clipped = jnp.clip(table_index, 0, table_blocks - 1)
    key_sel = key_table[clipped]
    value_sel = value_table[clipped]
    scores = (
        jnp.einsum("bqgd,bgskd->bgqsk", query_blocks, key_sel, preferred_element_type=jnp.float32)
        * scaling
    )
    position = jnp.arange(width)
    causal = position[:, None] >= position[None, :]
    allowed = usable[:, :, None, :, None] & (
        (offsets != 0)[:, :, None, :, None] | causal[None, None, :, None, :]
    )
    probability = jnp.where(allowed, jnp.exp(scores - log_part[:, :, :, None, None]), 0.0)
    prob_grad = jnp.einsum(
        "bqgd,bgskd->bgqsk", grad_blocks, value_sel, preferred_element_type=jnp.float32
    )
    score_grad = probability * (prob_grad - delta_part[:, :, :, None, None])
    prob_half = probability.astype(jnp.bfloat16)
    grad_half = score_grad.astype(jnp.bfloat16)
    query_grad = (
        jnp.einsum("bgqsk,bgskd->bqgd", grad_half, key_sel, preferred_element_type=jnp.float32)
        * scaling
    )
    key_terms = (
        jnp.einsum("bgqsk,bqgd->bgskd", grad_half, query_blocks, preferred_element_type=jnp.float32)
        * scaling
    )
    value_terms = jnp.einsum(
        "bgqsk,bqgd->bgskd", prob_half, grad_blocks, preferred_element_type=jnp.float32
    )
    onehot = (usable[..., None] & (clipped[..., None] == jnp.arange(table_blocks))).astype(
        jnp.float32
    )
    key_grad = jnp.einsum("bgsc,bgskd->ckd", onehot, key_terms, precision=lax.Precision.HIGHEST)
    value_grad = jnp.einsum("bgsc,bgskd->ckd", onehot, value_terms, precision=lax.Precision.HIGHEST)
    return (query_grad, key_grad, value_grad)


def per_device(
    queries,
    key_rows,
    value_rows,
    attn_out,
    out_grad,
    log_sums,
    block_picks,
    query_weight,
    key_weight,
    value_weight,
):
    tokens, query_cols = queries.shape
    head_dim = key_rows.shape[1]
    group = query_cols // head_dim
    width = BLK
    blocks = tokens // width
    cycle_pos = lax.axis_index("ctx")
    own_first = cycle_pos * blocks
    query_blocks = queries.reshape(blocks, width, group, head_dim)
    grad_blocks = out_grad.reshape(blocks, width, group, head_dim)
    delta_part = jnp.sum(
        (out_grad.astype(jnp.float32) * attn_out.astype(jnp.float32)).reshape(
            blocks, width, group, head_dim
        ),
        axis=3,
    ).transpose(0, 2, 1)
    log_part = log_sums.reshape(group, blocks, width).transpose(1, 0, 2)
    fetched = []
    for distance in (1, 2):
        fetched.append(passed_along((key_rows, value_rows), "ctx", distance))
    key_table = jnp.concatenate([fetched[1][0], fetched[0][0], key_rows], axis=0).reshape(
        3 * blocks, width, head_dim
    )
    value_table = jnp.concatenate([fetched[1][1], fetched[0][1], value_rows], axis=0).reshape(
        3 * blocks, width, head_dim
    )
    query_grad, key_grad, value_grad = block_grads(
        query_blocks,
        grad_blocks,
        log_part,
        delta_part,
        block_picks,
        own_first,
        key_table,
        value_table,
        own_first - 2 * blocks,
    )
    key_own = key_grad[2 * blocks :]
    value_own = value_grad[2 * blocks :]
    for distance in (1, 2):
        lower = (2 - distance) * blocks
        returned = passed_along(
            (key_grad[lower : lower + blocks], value_grad[lower : lower + blocks]), "ctx", -distance
        )
        key_own = key_own + returned[0]
        value_own = value_own + returned[1]
    grads = jnp.concatenate(
        [
            query_grad.reshape(tokens, query_cols).astype(jnp.bfloat16),
            key_own.reshape(tokens, head_dim).astype(jnp.bfloat16),
            value_own.reshape(tokens, head_dim).astype(jnp.bfloat16),
        ],
        axis=1,
    )
    weight_cat = jnp.concatenate([query_weight, key_weight, value_weight], axis=1)
    partial_value = lax.dot_general(
        grads,
        lax.all_gather(weight_cat, "ctx", axis=0, tiled=True),
        (((1,), (1,)), ((), ())),
        preferred_element_type=jnp.float32,
    )
    return lax.psum_scatter(
        partial_value.astype(jnp.bfloat16), "head", scatter_dimension=1, tiled=True
    )


def solution(mesh):
    placed = (
        P("ctx", "head"),
        P("ctx", "head"),
        P("ctx", "head"),
        P("ctx", "head"),
        P("ctx", "head"),
        P("head", "ctx"),
        P("ctx", "head", None),
        P("ctx", "head"),
        P("ctx", "head"),
        P("ctx", "head"),
    )
    return jax.shard_map(
        per_device, mesh=mesh, in_specs=placed, out_specs=P("ctx", "head"), check_vma=False
    )
```

profile of v0, /device:TPU:0, one launch (start us, length us, event | category | flops | bytes accessed | tf_op | source)
XLA Modules:
  0.0 122.5 jit_solution(4683026679644020689)
XLA Ops:
  6.5 1.8 %pad_maximum_fusion = bf16[256,768]{1,0:T(8,128)(2,1)} fusion(bf16[256,128]{1,0:T(8,128)(2,1)} %param.19, bf16[256,128]{1,0:T(8,128)(2,1)} %param.18, bf16[256,512]{1,0:T(8,128)(2,1)} %param.17), kind=kLoop, calls=%fused_computation.25 | loop fusion | flops 1179648 | bytes 786432 | tf_op jit(solution)/shard_map/concatenate | solution.py:139
  8.4 0.0 all-gather.2.cloned.1.call-update
  8.4 0.0 copy-start.2
  8.4 0.0 reduce-scatter.2.cloned.1.call-start
  8.5 4.8 %collective-permute-start = (bf16[256,128]{1,0:T(8,128)(2,1)}, bf16[256,128]{1,0:T(8,128)(2,1)S(1)}, u32[]{:S(2)}, u32[]{:S(2)}) collective-permute-start(bf16[256,128]{1,0:T(8,128)(2,1)} %param.11), channel_id=1, source_target_pairs={{0,4},{2,6},{4,8},{6,10},{8,12},{10,14},{12,16},{14,18},{16,20},{1... | collective-permute-start | bytes 196616 | tf_op jit(solution)/shard_map/ppermute | solution.py:14
  13.3 1.5 %collective-permute-start.1 = (bf16[256,128]{1,0:T(8,128)(2,1)}, bf16[256,128]{1,0:T(8,128)(2,1)S(1)}, u32[]{:S(2)}, u32[]{:S(2)}) collective-permute-start(bf16[256,128]{1,0:T(8,128)(2,1)} %param.11), channel_id=1, source_target_pairs={{0,2},{2,4},{4,6},{6,8},{8,10},{10,12},{12,14},{14,16},{16,18},{18... | collective-permute-start | bytes 196616 | tf_op jit(solution)/shard_map/ppermute | solution.py:14
  14.8 3.9 %collective-permute-start.2 = (bf16[256,128]{1,0:T(8,128)(2,1)}, bf16[256,128]{1,0:T(8,128)(2,1)S(1)}, u32[]{:S(2)}, u32[]{:S(2)}) collective-permute-start(bf16[256,128]{1,0:T(8,128)(2,1)} %param.12), channel_id=1, source_target_pairs={{0,4},{2,6},{4,8},{6,10},{8,12},{10,14},{12,16},{14,18},{16,20},{1... | collective-permute-start | bytes 196616 | tf_op jit(solution)/shard_map/ppermute | solution.py:14
  18.7 3.2 %collective-permute-start.3 = (bf16[256,128]{1,0:T(8,128)(2,1)}, bf16[256,128]{1,0:T(8,128)(2,1)S(1)}, u32[]{:S(2)}, u32[]{:S(2)}) collective-permute-start(bf16[256,128]{1,0:T(8,128)(2,1)} %param.12), channel_id=1, source_target_pairs={{0,2},{2,4},{4,6},{6,8},{8,10},{10,12},{12,14},{14,16},{16,18},{18... | collective-permute-start | bytes 196616 | tf_op jit(solution)/shard_map/ppermute | solution.py:14
  22.0 0.7 broadcast_add_fusion
  22.7 0.1 compare_select_fusion
  22.7 0.1 copy.38
  22.8 0.1 reshape.54
  22.9 0.1 compare_and_fusion
  23.0 0.1 copy.40
  23.1 0.1 copy.41
  23.2 1.0 reshape.47
  24.3 1.0 reshape.50
  25.3 0.1 convert_multiply_fusion
  25.4 0.0 copy-start.3
  25.4 0.2 reshape.51
  25.6 0.3 reduce_sum.9
  25.9 0.1 copy.46
  26.0 0.1 copy.50
  26.2 0.0 copy-start.4
  26.2 0.7 gather_fusion
  27.0 0.7 gather_fusion.1
  27.8 0.7 bitcast_select_fusion
  28.5 0.5 fusion
  29.0 0.4 convolution_multiply_fusion
  29.4 3.3 %fusion.5 = f32[6,128,128]{2,0,1:T(8,128)S(1)} fusion(f32[2,4,4,128,128]{4,3,2,1,0:T(8,128)S(1)} %convolution_multiply_fusion, s32[2,4,4]{2,1,0:T(4,128)S(1)} %copy.50, pred[2,4,4]{2,1,0:T(4,128)(4,1)S(1)} %copy.40), kind=kOutput, calls=%fused_computation.11 | convolution fusion | flops 37749120 | bytes 2490528 | tf_op jit(solution)/shard_map/bgsc,bgskd->ckd/dot_general | solution.py:69
  32.7 0.1 fusion.34
  32.8 1.3 %collective-permute-start.4 = (f32[2,128,128]{2,0,1:T(2,128)S(1)}, f32[2,128,128]{2,0,1:T(2,128)S(1)}, u32[]{:S(2)}, u32[]{:S(2)}) collective-permute-start(f32[2,128,128]{2,0,1:T(2,128)S(1)} %get-tuple-element.7), channel_id=1, source_target_pairs={{2,0},{4,2},{6,4},{8,6},{10,8},{12,10},{14,12},{16,14},{18,16},{20... | collective-permute-start | bytes 393224 | tf_op jit(solution)/shard_map/ppermute | solution.py:14
  34.1 1.3 %collective-permute-start.5 = (f32[2,128,128]{2,0,1:T(2,128)S(1)}, f32[2,128,128]{2,0,1:T(2,128)S(1)}, u32[]{:S(2)}, u32[]{:S(2)}) collective-permute-start(f32[2,128,128]{2,0,1:T(2,128)S(1)} %get-tuple-element.8), channel_id=1, source_target_pairs={{4,0},{6,2},{8,4},{10,6},{12,8},{14,10},{16,12},{18,14},{20,16},{2... | collective-permute-start | bytes 393224 | tf_op jit(solution)/shard_map/ppermute | solution.py:14
  35.4 0.4 fusion.14
  35.9 3.3 %fusion.8 = f32[6,128,128]{2,0,1:T(8,128)S(1)} fusion(f32[2,4,4,128,128]{4,3,2,1,0:T(8,128)S(1)} %fusion.14, s32[2,4,4]{2,1,0:T(4,128)S(1)} %copy.50, pred[2,4,4]{2,1,0:T(4,128)(4,1)S(1)} %copy.40), kind=kOutput, calls=%fused_computation.12 | convolution fusion | flops 37749120 | bytes 2490528 | tf_op jit(solution)/shard_map/bgsc,bgskd->ckd/dot_general | solution.py:70
  39.2 0.5 fusion.13
  39.7 0.1 fusion.35
  39.8 1.3 %collective-permute-start.6 = (f32[2,128,128]{2,0,1:T(2,128)S(1)}, f32[2,128,128]{2,0,1:T(2,128)S(1)}, u32[]{:S(2)}, u32[]{:S(2)}) collective-permute-start(f32[2,128,128]{2,0,1:T(2,128)S(1)} %get-tuple-element.9), channel_id=1, source_target_pairs={{2,0},{4,2},{6,4},{8,6},{10,8},{12,10},{14,12},{16,14},{18,16},{20... | collective-permute-start | bytes 393224 | tf_op jit(solution)/shard_map/ppermute | solution.py:14
  41.1 1.3 %collective-permute-start.7 = (f32[2,128,128]{2,0,1:T(2,128)S(1)}, f32[2,128,128]{2,0,1:T(2,128)S(1)}, u32[]{:S(2)}, u32[]{:S(2)}) collective-permute-start(f32[2,128,128]{2,0,1:T(2,128)S(1)} %get-tuple-element.10), channel_id=1, source_target_pairs={{4,0},{6,2},{8,4},{10,6},{12,8},{14,10},{16,12},{18,14},{20,16},{2... | collective-permute-start | bytes 393224 | tf_op jit(solution)/shard_map/ppermute | solution.py:14
  42.4 0.2 copy.48
  42.6 0.1 fusion.28
  42.8 1.0 collective-permute-done.6
  43.8 12.3 %collective-permute-done.7 = f32[2,128,128]{2,0,1:T(2,128)S(1)} collective-permute-done((f32[2,128,128]{2,0,1:T(2,128)S(1)}, f32[2,128,128]{2,0,1:T(2,128)S(1)}, u32[]{:S(2)}, u32[]{:S(2)}) %collective-permute-start.7) | collective-permute-done | bytes 131104 | tf_op jit(solution)/shard_map/ppermute | solution.py:14
  56.1 0.1 fusion.26
  56.3 22.8 %all-gather.2.cloned.1.call-done = bf16[4096,768]{1,0:T(8,128)(2,1)} async-done(((bf16[256,768]{1,0:T(8,128)(2,1)}), bf16[4096,768]{1,0:T(8,128)(2,1)}) %all-gather.2.cloned.1.call-update) | async-done | bytes 6291472 | tf_op jit(solution)/shard_map/all_gather | solution.py:142
  79.1 6.0 %convolution_convert_fusion = bf16[256,4096]{1,0:T(8,128)(2,1)} fusion(bf16[4096,768]{1,0:T(8,128)(2,1)} %all-gather.2.cloned.1.call-done, bf16[256,128]{1,0:T(8,128)(2,1)S(1)} %bitcast.71, bf16[256,128]{1,0:T(8,128)(2,1)S(1)} %bitcast.70, bf16[256,512]{1,0:T(8,128)(2,1)S(1)} %bitcast.69), kind=kOutput, calls=%fused_computation.2 | convolution fusion | flops 1612840960 | bytes 8781824 | tf_op jit(solution)/shard_map/dot_general | solution.py:140
  85.1 0.0 reduce-scatter.2.cloned.1.call-update
  85.1 30.6 %reduce-scatter.2.cloned.1.call-done = bf16[256,2048]{1,0:T(8,128)(2,1)} async-done(((bf16[256,4096]{1,0:T(8,128)(2,1)}), bf16[256,2048]{1,0:T(8,128)(2,1)}) %reduce-scatter.2.cloned.1.call-update) | async-done | bytes 1048592 | tf_op jit(solution)/shard_map/reduce_scatter | solution.py:146
  (22 shorter events, 0.2 us)
Async XLA Ops:
  6.5 18.8 %copy-start = (bf16[256,512]{1,0:T(8,128)(2,1)S(1)}, bf16[256,512]{1,0:T(8,128)(2,1)}, u32[]{:S(2)}) copy-start(bf16[256,512]{1,0:T(8,128)(2,1)} %param.14) | copy-start | bytes 786436
  6.5 18.8 %copy-start.1 = (bf16[256,512]{1,0:T(8,128)(2,1)S(1)}, bf16[256,512]{1,0:T(8,128)(2,1)}, u32[]{:S(2)}) copy-start(bf16[256,512]{1,0:T(8,128)(2,1)} %param.13) | copy-start | bytes 786436
  6.5 72.5 %all-gather.2.cloned.1.call-start = ((), (), s32[]{:S(2)}) async-start(), calls=%async_computation.1 | async-start | bytes 6684672 | tf_op jit(solution)/shard_map/all_gather | solution.py:142
  8.4 17.8 %copy-start.2 = (bf16[256,128]{1,0:T(8,128)(2,1)S(1)}, bf16[256,128]{1,0:T(8,128)(2,1)}, u32[]{:S(2)}) copy-start(bf16[256,128]{1,0:T(8,128)(2,1)} %param.11) | copy-start | bytes 196612
  8.4 107.2 %reduce-scatter.2.cloned.1.call-start = ((), (), s32[]{:S(2)}) async-start(), calls=%async_computation.2 | async-start | bytes 3145728 | tf_op jit(solution)/shard_map/reduce_scatter | solution.py:146
  8.5 17.7 %collective-permute-start = (bf16[256,128]{1,0:T(8,128)(2,1)}, bf16[256,128]{1,0:T(8,128)(2,1)S(1)}, u32[]{:S(2)}, u32[]{:S(2)}) collective-permute-start(bf16[256,128]{1,0:T(8,128)(2,1)} %param.11), channel_id=1, source_target_pairs={{0,4},{2,6},{4,8},{6,10},{8,12},{10,14},{12,16},{14,18},{16,20},{1... | collective-permute-start | bytes 196616 | tf_op jit(solution)/shard_map/ppermute | solution.py:14
  13.3 12.8 %collective-permute-start.1 = (bf16[256,128]{1,0:T(8,128)(2,1)}, bf16[256,128]{1,0:T(8,128)(2,1)S(1)}, u32[]{:S(2)}, u32[]{:S(2)}) collective-permute-start(bf16[256,128]{1,0:T(8,128)(2,1)} %param.11), channel_id=1, source_target_pairs={{0,2},{2,4},{4,6},{6,8},{8,10},{10,12},{12,14},{14,16},{16,18},{18... | collective-permute-start | bytes 196616 | tf_op jit(solution)/shard_map/ppermute | solution.py:14
  14.8 12.2 %collective-permute-start.2 = (bf16[256,128]{1,0:T(8,128)(2,1)}, bf16[256,128]{1,0:T(8,128)(2,1)S(1)}, u32[]{:S(2)}, u32[]{:S(2)}) collective-permute-start(bf16[256,128]{1,0:T(8,128)(2,1)} %param.12), channel_id=1, source_target_pairs={{0,4},{2,6},{4,8},{6,10},{8,12},{10,14},{12,16},{14,18},{16,20},{1... | collective-permute-start | bytes 196616 | tf_op jit(solution)/shard_map/ppermute | solution.py:14
  18.7 8.3 %collective-permute-start.3 = (bf16[256,128]{1,0:T(8,128)(2,1)}, bf16[256,128]{1,0:T(8,128)(2,1)S(1)}, u32[]{:S(2)}, u32[]{:S(2)}) collective-permute-start(bf16[256,128]{1,0:T(8,128)(2,1)} %param.12), channel_id=1, source_target_pairs={{0,2},{2,4},{4,6},{6,8},{8,10},{10,12},{12,14},{14,16},{16,18},{18... | collective-permute-start | bytes 196616 | tf_op jit(solution)/shard_map/ppermute | solution.py:14
  25.4 1.6 %copy-start.3 = (bf16[256,128]{1,0:T(8,128)(2,1)S(1)}, bf16[256,128]{1,0:T(8,128)(2,1)}, u32[]{:S(2)}) copy-start(bf16[256,128]{1,0:T(8,128)(2,1)} %param.12) | copy-start | bytes 196612
  26.2 1.6 %copy-start.4 = (f32[4,256]{1,0:T(4,128)S(1)}, f32[4,256]{1,0:T(4,128)}, u32[]{:S(2)}) copy-start(f32[4,256]{1,0:T(4,128)} %param.15) | copy-start | bytes 12292
  32.8 9.8 %collective-permute-start.4 = (f32[2,128,128]{2,0,1:T(2,128)S(1)}, f32[2,128,128]{2,0,1:T(2,128)S(1)}, u32[]{:S(2)}, u32[]{:S(2)}) collective-permute-start(f32[2,128,128]{2,0,1:T(2,128)S(1)} %get-tuple-element.7), channel_id=1, source_target_pairs={{2,0},{4,2},{6,4},{8,6},{10,8},{12,10},{14,12},{16,14},{18,16},{20... | collective-permute-start | bytes 393224 | tf_op jit(solution)/shard_map/ppermute | solution.py:14
  34.1 8.5 %collective-permute-start.5 = (f32[2,128,128]{2,0,1:T(2,128)S(1)}, f32[2,128,128]{2,0,1:T(2,128)S(1)}, u32[]{:S(2)}, u32[]{:S(2)}) collective-permute-start(f32[2,128,128]{2,0,1:T(2,128)S(1)} %get-tuple-element.8), channel_id=1, source_target_pairs={{4,0},{6,2},{8,4},{10,6},{12,8},{14,10},{16,12},{18,14},{20,16},{2... | collective-permute-start | bytes 393224 | tf_op jit(solution)/shard_map/ppermute | solution.py:14
  39.8 4.1 %collective-permute-start.6 = (f32[2,128,128]{2,0,1:T(2,128)S(1)}, f32[2,128,128]{2,0,1:T(2,128)S(1)}, u32[]{:S(2)}, u32[]{:S(2)}) collective-permute-start(f32[2,128,128]{2,0,1:T(2,128)S(1)} %get-tuple-element.9), channel_id=1, source_target_pairs={{2,0},{4,2},{6,4},{8,6},{10,8},{12,10},{14,12},{16,14},{18,16},{20... | collective-permute-start | bytes 393224 | tf_op jit(solution)/shard_map/ppermute | solution.py:14
  41.1 15.0 %collective-permute-start.7 = (f32[2,128,128]{2,0,1:T(2,128)S(1)}, f32[2,128,128]{2,0,1:T(2,128)S(1)}, u32[]{:S(2)}, u32[]{:S(2)}) collective-permute-start(f32[2,128,128]{2,0,1:T(2,128)S(1)} %get-tuple-element.10), channel_id=1, source_target_pairs={{4,0},{6,2},{8,4},{10,6},{12,8},{14,10},{16,12},{18,14},{20,16},{2... | collective-permute-start | bytes 393224 | tf_op jit(solution)/shard_map/ppermute | solution.py:14
Sparse Core Ops, SparseCore 0:
  9.6 69.3 all-gather.1
  85.2 30.4 reduce-scatter.1
where the time goes:
time: 123 us; the launch traced here: 122 us
  waiting for transfers between devices  66.7 us (54%)
  starting transfers between devices  18.7 us (15%)
  matrix products  15.1 us (12%)
  between operations  13.8 us (11%)
  local copies, waits for them, and re-layouts  4.79 us (4%)
  other arithmetic  3.43 us (3%)
    reduce_scatter x1, waiting for transfers between devices, per_device(): lax.psum_scatter(partial_value.astype(jnp.bfloat16), 'head', scatter_dime...  30.6 us
    all_gather x1, waiting for transfers between devices, per_device(): lax.all_gather(weight_cat, 'ctx', axis=0, tiled=True)  22.8 us
    ppermute x8, starting transfers between devices, passed_along(): return lax.ppermute(x, axis, pairs)  18.6 us
    ppermute x8, waiting for transfers between devices, passed_along(): return lax.ppermute(x, axis, pairs)  13.3 us
    dot_general x1, matrix products, per_device(): lax.dot_general(grads, lax.all_gather(weight_cat, 'ctx', axis=0, tiled=Tr...  5.98 us
    dot_general x1, matrix products, block_grads(): jnp.einsum('bgsc,bgskd->ckd', onehot, value_terms, precision=lax.Precisio...  3.3 us
    dot_general x1, matrix products, block_grads(): jnp.einsum('bgsc,bgskd->ckd', onehot, key_terms, precision=lax.Precision....  3.3 us
  transfers between devices with their start and end apart: 10, of which 4 were waited for; matrix products, arithmetic and copies ran while one was open for 13% of the time, Pallas kernels for 0%

commit v1 on v0

v1 whole, which is shorter than its diff:
```python
import functools
import math

import jax
import jax.numpy as jnp
from jax import lax
from jax.experimental import pallas as pl
from jax.experimental.pallas import tpu as pltpu
from jax.sharding import PartitionSpec as P

BLK = 128
WINDOW = 4
MESH = pl.DeviceIdType.MESH
NEG = -1e30


def dot_nt(a, b):
    return lax.dot_general(a, b, (((1,), (1,)), ((), ())), preferred_element_type=jnp.float32)


def dot_nn(a, b):
    return lax.dot_general(a, b, (((1,), (0,)), ((), ())), preferred_element_type=jnp.float32)


def kernel(
    ctx, heads, group, hd, far,
    q_hbm, k_hbm, v_hbm, o_hbm, g_hbm, lse_ref, picks_ref, wq_hbm, wk_hbm, wv_hbm,
    out_ref,
    w, q, g, o, kv, pt, dst, acc, ksend, krecv, grads, part, got,
    local_sem, halo_send, halo_recv, back_send, back_recv,
    ring_send, ring_recv, sib_send, sib_recv, part_send, part_recv,
):
    i = lax.axis_index("ctx")
    me = lax.axis_index("head")
    tokens = q.shape[0]
    blocks = tokens // BLK
    rows = w.shape[1]
    half = rows // 2
    cols = group * hd
    scaling = 1.0 / math.sqrt(hd)
    chips = ctx // 2
    depth = chips // 2
    steps = chips // 2
    core = i % 2
    chip = i // 2
    side = chip % 2
    at = (chip // 2) * (1 - side) + (chips - 1 - chip // 2) * side

    def owner(pos):
        pos = (pos + chips) % chips
        high = pos // depth
        return 2 * ((1 - high) * 2 * pos + high * (2 * (chips - 1 - pos) + 1)) + core

    up, down = owner(at + 1), owner(at - 1)
    sibling = i + 1 - 2 * core

    local = [
        pltpu.make_async_copy(wq_hbm, w.at[i, :, pl.ds(0, cols)], local_sem.at[0]),
        pltpu.make_async_copy(wk_hbm, w.at[i, :, pl.ds(cols, hd)], local_sem.at[1]),
        pltpu.make_async_copy(wv_hbm, w.at[i, :, pl.ds(cols + hd, hd)], local_sem.at[2]),
        pltpu.make_async_copy(k_hbm, kv.at[far, 0], local_sem.at[3]),
        pltpu.make_async_copy(v_hbm, kv.at[far, 1], local_sem.at[4]),
        pltpu.make_async_copy(q_hbm, q, local_sem.at[5]),
        pltpu.make_async_copy(g_hbm, g, local_sem.at[6]),
        pltpu.make_async_copy(o_hbm, o, local_sem.at[7]),
    ]
    for copy in (local[3], local[4], *local[:3], *local[5:]):
        copy.start()

    barrier = pltpu.get_barrier_semaphore()
    peers = [(up, me), (down, me), (sibling, me)]
    for d in range(1, far + 1):
        peers += [((i + d) % ctx, me), ((i + ctx - d) % ctx, me)]
    for d in range(1, heads):
        peers.append((i, (me + d) % heads))
    for peer in peers:
        pl.semaphore_signal(barrier, inc=1, device_id=peer, device_id_type=MESH)
    for d in range(1, far + 1):

        @pl.when(i < d)
        def _():
            kv[far - d] = jnp.zeros_like(kv[far - d])

        @pl.when(i + d >= ctx)
        def _():
            krecv[d - 1] = jnp.zeros_like(krecv[d - 1])

    pl.semaphore_wait(barrier, len(peers))

    def remote(src, dest, ssem, rsem, to):
        return pltpu.make_async_remote_copy(
            src_ref=src, dst_ref=dest, send_sem=ssem, recv_sem=rsem,
            device_id=to, device_id_type=MESH,
        )

    def halo(d):
        return remote(kv.at[far], kv.at[far - d], halo_send.at[d - 1], halo_recv.at[d - 1],
                      ((i + d) % ctx, me))

    def back(d):
        return remote(ksend.at[d - 1], krecv.at[d - 1], back_send.at[d - 1], back_recv.at[d - 1],
                      ((i + ctx - d) % ctx, me))

    def ring(way, step, piece, shard):
        ref = w.at[shard, pl.ds(piece * half, half)]
        return remote(ref, ref, ring_send.at[way, step - 1, piece], ring_recv.at[way, step - 1, piece],
                      (up if way == 0 else down, me))

    def share(slot, shard):
        return remote(w.at[shard], w.at[shard], sib_send.at[slot], sib_recv.at[slot], (sibling, me))

    def pieces(way, step):
        return (0, 1) if step < steps else (way,)

    def source(way, step):
        return owner(at - step) if way == 0 else owner(at + step)

    def other(shard):
        return shard + 1 - 2 * core

    local[3].wait()
    local[4].wait()
    for d in range(1, far + 1):

        @pl.when(i + d < ctx)
        def _():
            halo(d).start()

    for copy in local[:3]:
        copy.wait()
    for piece in (0, 1):
        for way in (0, 1):
            if piece in pieces(way, 1):
                ring(way, 1, piece, i).start()
    share(0, i).start()
    for copy in local[5:]:
        copy.wait()

    acc[...] = jnp.zeros_like(acc)
    for d in range(1, far + 1):

        @pl.when(i >= d)
        def _():
            halo(d).wait_recv()

    first = far * blocks - WINDOW
    row_id = lax.broadcasted_iota(jnp.int32, (BLK, BLK), 0)
    col_id = lax.broadcasted_iota(jnp.int32, (BLK, BLK), 1)
    causal_one = row_id <= col_id
    causal = jnp.concatenate([causal_one] * group, axis=1)

    def table(which, block):
        return kv[block // blocks, which, pl.ds((block % blocks) * BLK, BLK), :]

    for b in range(blocks):
        span = pl.ds(b * BLK, BLK)
        qs = jnp.concatenate([q[span, pl.ds(h * hd, hd)] for h in range(group)], axis=0)
        gs = jnp.concatenate([g[span, pl.ds(h * hd, hd)] for h in range(group)], axis=0)
        delta = jnp.concatenate(
            [
                jnp.sum(
                    (
                        g[span, pl.ds(h * hd, hd)].astype(jnp.float32)
                        * o[span, pl.ds(h * hd, hd)].astype(jnp.float32)
                    ).T,
                    axis=0,
                    keepdims=True,
                )
                for h in range(group)
            ],
            axis=1,
        )
        for m in range(WINDOW + 1):
            away = WINDOW - m
            shifts = []
            for h in range(group):
                piece = -lse_ref[pl.ds(h, 1), span]
                if away:
                    hit = picks_ref[b, h, 0] == away - 1
                    for c in range(1, picks_ref.shape[2]):
                        hit = jnp.logical_or(hit, picks_ref[b, h, c] == away - 1)
                    hit = jnp.logical_and(hit, i * blocks + b >= away)
                    piece = piece + jnp.where(hit, 0.0, NEG)
                shifts.append(piece)
            shift = jnp.concatenate(shifts, axis=1)
            key = table(0, first + b + m)
            value = table(1, first + b + m)
            p = jnp.exp(dot_nt(key, qs) * scaling + shift)
            if not away:
                p = jnp.where(causal, p, 0.0)
            ds = p * (dot_nt(value, gs) - delta)
            pt[pl.ds(m * BLK, BLK), :] = p.astype(jnp.bfloat16)
            dst[pl.ds(m * BLK, BLK), :] = ds.astype(jnp.bfloat16)
        window = pl.ds((first + b) * BLK, (WINDOW + 1) * BLK)
        dsv = dst[...]
        acc[0, window, :] += dot_nn(dsv, qs)
        acc[1, window, :] += dot_nn(pt[...], gs)
        keys_t = jnp.concatenate(
            [table(0, first + b + m) for m in range(WINDOW + 1)], axis=0
        ).T
        dq = dot_nn(keys_t, dsv) * scaling
        for h in range(group):
            grads[span, pl.ds(h * hd, hd)] = dq[:, h * BLK : (h + 1) * BLK].T.astype(jnp.bfloat16)

    for d in range(1, far + 1):
        span = pl.ds((far - d) * tokens, tokens)
        ksend[d - 1, 0] = (acc[0, span, :] * scaling).astype(jnp.bfloat16)
        ksend[d - 1, 1] = acc[1, span, :].astype(jnp.bfloat16)

        @pl.when(i >= d)
        def _():
            back(d).start()

    def advance(step):
        for piece in (0, 1):
            for way in (0, 1):
                if piece in pieces(way, step):
                    shard = source(way, step)
                    ring(way, step, piece, shard).wait_recv()
                    if step < steps and piece in pieces(way, step + 1):
                        ring(way, step + 1, piece, shard).start()
        for way in (0, 1) if step < steps else (0,):
            share(2 * step - 1 + way, source(way, step)).start()

    advance(1)

    for d in range(1, far + 1):

        @pl.when(i + d < ctx)
        def _():
            back(d).wait_recv()

    own = pl.ds(far * tokens, tokens)
    dk = acc[0, own, :] * scaling
    dv = acc[1, own, :]
    for d in range(1, far + 1):
        dk += krecv[d - 1, 0].astype(jnp.float32)
        dv += krecv[d - 1, 1].astype(jnp.float32)
    grads[:, pl.ds(cols, hd)] = dk.astype(jnp.bfloat16)
    grads[:, pl.ds(cols + hd, hd)] = dv.astype(jnp.bfloat16)

    per = ctx // heads

    def handing(shard):
        return remote(part.at[shard], got.at[me, shard % per], part_send.at[shard],
                      part_recv.at[me, shard % per], (i, shard // per))

    def project(shard):
        part[shard] = dot_nt(grads[...], w[shard]).astype(jnp.bfloat16)

        @pl.when(shard // per != me)
        def _():
            handing(shard).start()

    project(i)
    share(0, other(i)).wait_recv()
    project(other(i))
    for step in range(1, steps + 1):
        ways = (0, 1) if step < steps else (0,)
        if step > 1:
            advance(step)
        for way in ways:
            project(source(way, step))
        for way in ways:
            shard = other(source(way, step))
            share(2 * step - 1 + way, shard).wait_recv()
            project(shard)

    for l in range(per):
        total = part[me * per + l].astype(jnp.float32)
        for d in range(1, heads):
            giver = (me + d) % heads
            remote(got.at[giver, l], got.at[giver, l], part_send.at[0], part_recv.at[giver, l],
                   (i, giver)).wait_recv()
            total += got[giver, l].astype(jnp.float32)
        out_ref[:, pl.ds(l * rows, rows)] = total.astype(jnp.bfloat16)

    for d in range(1, far + 1):

        @pl.when(i + d < ctx)
        def _():
            halo(d).wait_send()

        @pl.when(i >= d)
        def _():
            back(d).wait_send()

    for step in range(1, steps + 1):
        for way in (0, 1):
            for piece in pieces(way, step):
                ring(way, step, piece, source(way, step - 1)).wait_send()
    for slot in range(2 * steps):
        share(slot, i).wait_send()
    for shard in range(ctx):

        @pl.when(shard // per != me)
        def _():
            handing(shard).wait_send()


def per_device(ctx, heads, queries, key_rows, value_rows, attn_out, out_grad, log_sums,
               block_picks, query_weight, key_weight, value_weight):
    tokens, cols = queries.shape
    hd = key_rows.shape[1]
    group = cols // hd
    blocks = tokens // BLK
    far = -(-WINDOW // blocks)
    rows = query_weight.shape[0]
    width = cols + 2 * hd
    steps = ctx // 4
    per = ctx // heads
    bf, f32 = jnp.bfloat16, jnp.float32
    dma = pltpu.SemaphoreType.DMA
    hbm = pl.BlockSpec(memory_space=pl.ANY)
    return pl.pallas_call(
        functools.partial(kernel, ctx, heads, group, hd, far),
        out_shape=jax.ShapeDtypeStruct((tokens, per * rows), bf),
        in_specs=[hbm] * 5
        + [pl.BlockSpec(memory_space=pltpu.VMEM), pl.BlockSpec(memory_space=pltpu.SMEM)]
        + [hbm] * 3,
        out_specs=pl.BlockSpec(memory_space=pltpu.VMEM),
        scratch_shapes=[
            pltpu.VMEM((ctx, rows, width), bf),
            pltpu.VMEM((tokens, cols), bf),
            pltpu.VMEM((tokens, cols), bf),
            pltpu.VMEM((tokens, cols), bf),
            pltpu.VMEM((far + 1, 2, tokens, hd), bf),
            pltpu.VMEM(((WINDOW + 1) * BLK, group * BLK), bf),
            pltpu.VMEM(((WINDOW + 1) * BLK, group * BLK), bf),
            pltpu.VMEM((2, (far + 1) * tokens, hd), f32),
            pltpu.VMEM((far, 2, tokens, hd), bf),
            pltpu.VMEM((far, 2, tokens, hd), bf),
            pltpu.VMEM((tokens, width), bf),
            pltpu.VMEM((ctx, tokens, rows), bf),
            pltpu.VMEM((heads, per, tokens, rows), bf),
            dma((8,)), dma((far,)), dma((far,)), dma((far,)), dma((far,)),
            dma((2, steps, 2)), dma((2, steps, 2)),
            dma((2 * steps,)), dma((2 * steps,)),
            dma((ctx,)), dma((heads, per)),
        ],
        compiler_params=pltpu.CompilerParams(
            collective_id=0, has_side_effects=True, vmem_limit_bytes=56 * 1024 * 1024
        ),
    )(queries, key_rows, value_rows, attn_out, out_grad, log_sums, block_picks,
      query_weight, key_weight, value_weight)


def solution(mesh):
    placed = (
        P("ctx", "head"),
        P("ctx", "head"),
        P("ctx", "head"),
        P("ctx", "head"),
        P("ctx", "head"),
        P("head", "ctx"),
        P("ctx", "head", None),
        P("ctx", "head"),
        P("ctx", "head"),
        P("ctx", "head"),
    )
    body = functools.partial(per_device, mesh.shape["ctx"], mesh.shape["head"])
    return jax.shard_map(
        body, mesh=mesh, in_specs=placed, out_specs=P("ctx", "head"), check_vma=False
    )
```

time: 123 us -> 65.3 us (0.53)
  the two profiles are of different devices: /device:TPU:0 before, /device:TPU:7 now
where the time goes in v1:
time: 65.3 us; the launch traced here: 65.1 us
  Pallas kernels  61.4 us (94%)
  local copies, waits for them, and re-layouts  3.67 us (6%)
    pallas_call x1, Pallas kernels, per_device(): pl.pallas_call(functools.partial(kernel, ctx, heads, group, hd, far), out...  61.4 us
    unnamed x2, local copies, waits for them, and re-layouts  3.67 us

profile of v1, /device:TPU:7, one launch (start us, length us, event | category | flops | bytes accessed | tf_op | source)
XLA Modules:
  0.0 65.1 jit_solution(7084954569413112765)
XLA Ops:
  0.0 1.4 %copy.11.picks_ref = s32[2,4,3]{2,1,0:T(4,128)} copy(s32[2,4,3]{1,0,2:T(2,128)} %param.16) | data formatting | bytes 192 | tf_op args[6]
  1.4 61.4 %shard_map.100 = bf16[256,2048]{1,0:T(8,128)(2,1)} custom-call(bf16[256,512]{1,0:T(8,128)(2,1)} %q_hbm.1, bf16[256,128]{1,0:T(8,128)(2,1)} %k_hbm.1, bf16[256,128]{1,0:T(8,128)(2,1)} %v_hbm.1, bf16[256,512]{1,0:T(8,128)(2,1)} %o_hbm.1, bf16[256,512]{1,0:T(8,128)(2,1)} %g_hbm.1, f32[4,256]{1,0:T(4,128)} %lse_ref.1, s32[2,4,3]{2,1,0:T(4,128)} %copy.11.picks_ref, ...), custom_call_target="tpu_custom_call" | custom-call | tf_op jit(solution)/shard_map/pallas_call | solution.py:315
  62.8 2.3 %copy.13 = bf16[256,2048]{1,0:T(8,128)(2,1)} copy(bf16[256,2048]{1,0:T(8,128)(2,1)} %shard_map.100) | data formatting | bytes 2097152

commit v2 on v1

--- a/solution.py
+++ b/solution.py
@@ -128,10 +128,8 @@
 
     for copy in local[:3]:
         copy.wait()
-    for piece in (0, 1):
-        for way in (0, 1):
-            if piece in pieces(way, 1):
-                ring(way, 1, piece, i).start()
+    for way in (0, 1):
+        ring(way, 1, pieces(way, 1)[0], i).start()
     share(0, i).start()
     for copy in local[5:]:
         copy.wait()
@@ -222,6 +220,10 @@
         for way in (0, 1) if step < steps else (0,):
             share(2 * step - 1 + way, source(way, step)).start()
 
+    for way in (0, 1):
+        for piece in pieces(way, 1)[1:]:
+            ring(way, 1, piece, i).start()
+
     advance(1)
 
     for d in range(1, far + 1):

time: 65.3 us -> 64.8 us (level)
  no operation moved by 1% of the time
where the time goes in v2:
time: 64.8 us; the launch traced here: 64.6 us
  Pallas kernels  60.9 us (94%)
  local copies, waits for them, and re-layouts  3.67 us (6%)
    pallas_call x1, Pallas kernels, per_device(): pl.pallas_call(functools.partial(kernel, ctx, heads, group, hd, far), out...  60.9 us
    unnamed x2, local copies, waits for them, and re-layouts  3.67 us

profile of v2, /device:TPU:7, one launch (start us, length us, event | category | flops | bytes accessed | tf_op | source)
XLA Modules:
  0.0 64.6 jit_solution(1033761564234751578)
XLA Ops:
  0.0 1.4 %copy.11.picks_ref = s32[2,4,3]{2,1,0:T(4,128)} copy(s32[2,4,3]{1,0,2:T(2,128)} %param.16) | data formatting | bytes 192 | tf_op args[6]
  1.4 60.9 %shard_map.100 = bf16[256,2048]{1,0:T(8,128)(2,1)} custom-call(bf16[256,512]{1,0:T(8,128)(2,1)} %q_hbm.1, bf16[256,128]{1,0:T(8,128)(2,1)} %k_hbm.1, bf16[256,128]{1,0:T(8,128)(2,1)} %v_hbm.1, bf16[256,512]{1,0:T(8,128)(2,1)} %o_hbm.1, bf16[256,512]{1,0:T(8,128)(2,1)} %g_hbm.1, f32[4,256]{1,0:T(4,128)} %lse_ref.1, s32[2,4,3]{2,1,0:T(4,128)} %copy.11.picks_ref, ...), custom_call_target="tpu_custom_call" | custom-call | tf_op jit(solution)/shard_map/pallas_call | solution.py:317
  62.3 2.3 %copy.13 = bf16[256,2048]{1,0:T(8,128)(2,1)} copy(bf16[256,2048]{1,0:T(8,128)(2,1)} %shard_map.100) | data formatting | bytes 2097152
